TPU v7x, 256 devices: a whole 4x4x8 slice. The times are simulated.
256 devices in a mesh: pool: 64 (over y_lo, z, x), head: 4 (over y_hi, core).
Axes of the slice: x: 4, y: 4 (y_hi: 2, y_lo: 2; y = y_hi * 2 + y_lo), z: 8, core: 2. Of those that a mesh axis runs over, the one named last changes fastest.
Arguments:
- queries: bfloat16 [64, 8192], P('pool', 'head'), may hold values from -12 to 12
- new_kv: bfloat16 [64, 2, 1024], P('pool', None, 'head'), may hold values from -8 to 8
- cache_kv: bfloat16 [1024, 2, 8, 256, 128], P('pool', None, 'head'), may hold values from -6 to 6
- out_weight: bfloat16 [8192, 8192], P('head', 'pool'), may hold values from -0.0625 to 0.0625
- block_table: int32 [32, 32], replicated, may hold values from 0 to 1023, as said below
- home_slot: int32 [32], replicated, may hold values from 0 to 63, as said below
- block_counts: int32 [1024], replicated, may hold values from 1 to 256, as said below
- lengths: int32 [32], replicated, may hold values from 2 to 8192, as said below
Outputs:
- attn_out: float32 [32, 8192], P(None, ('pool', 'head'))
Inputs may be any that keep to these rules, and one draw needn't show every extreme that they name: `block_table`: every one of the 1024 blocks appears exactly once in the table; block b is held by pool device b // 16. `home_slot`: the slots are distinct; slot s belongs to pool device s. A block's valid tokens are its first block_counts positions; each request's first block has 2 or more. lengths[r] is at most the sum of block_counts over request r's blocks, and equal to that sum for at least one request.
All inputs are finite; a program needn't handle non-finite values.
Results may differ from a plain program's by a relative error of at most 0.005.
Values may be sent and summed in bfloat16 or wider, within the bound.
A program may use at most 128 MiB of HBM per device.

v0:
```python
import math

import jax
import jax.numpy as jnp
from jax import lax
from jax.sharding import PartitionSpec as P

floor_value = -1e30


def joined(value, axis, join):
    pieces = jax.tree.map(lambda part: lax.all_gather(part, axis), value)
    head = jax.tree.map(lambda part: part[0], pieces)
    tail = jax.tree.map(lambda part: part[1:], pieces)
    subtotal, _ = lax.scan(lambda subtotal, slab: (join(subtotal, slab), None), head, tail)
    return subtotal


def per_device(
    queries, new_kv, cache_kv, out_weight, block_table, home_slot, block_counts, lengths
):
    local_blocks, _, heads_here, block_len, head_dim = cache_kv.shape
    requests, list_len = block_table.shape
    slots_here = queries.shape[0]
    q_heads = queries.shape[1] // head_dim
    per_group = q_heads // heads_here
    score_scale = 1.0 / math.sqrt(head_dim)
    highest = lax.Precision.HIGHEST
    pool_index = lax.axis_index("pool")
    every_slot = lax.all_gather(queries, "pool", axis=0, tiled=True)
    query_all = every_slot[home_slot]
    block_ids = pool_index * local_blocks + jnp.arange(local_blocks, dtype=jnp.int32)
    flat_table = block_table.reshape(-1)
    matches = flat_table[None, :] == block_ids[:, None]
    entries = jnp.sum(
        jnp.where(matches, jnp.arange(flat_table.shape[0], dtype=jnp.int32)[None, :], 0), axis=1
    )
    owners = entries // list_len
    listed = block_counts[block_table]
    starts = jnp.cumsum(listed, axis=1) - listed
    block_start = starts[owners, entries % list_len]
    count_here = block_counts[block_ids]
    positions = jnp.arange(block_len, dtype=jnp.int32)
    live_mask = (positions[None, :] < count_here[:, None]) & (
        block_start[:, None] + positions[None, :] < lengths[owners][:, None]
    )
    query_grid = query_all.reshape(requests, heads_here, per_group, head_dim)
    block_query = query_grid[owners]
    scores = (
        jnp.einsum(
            "bgjd,bgtd->bgjt", block_query, cache_kv[:, 0], preferred_element_type=jnp.float32
        )
        * score_scale
    )
    scores = jnp.where(live_mask[:, None, None, :], scores, floor_value)
    block_top = jnp.max(scores, axis=-1)
    members = owners[:, None] == jnp.arange(requests, dtype=jnp.int32)[None, :]
    request_top = jnp.max(
        jnp.where(members[:, :, None, None], block_top[:, None], floor_value), axis=0
    )
    home_here = home_slot // slots_here == pool_index
    fresh_kv = new_kv[home_slot % slots_here].reshape(requests, 2, heads_here, head_dim)
    own_score = (
        jnp.einsum("rgjd,rgd->rgj", query_grid, fresh_kv[:, 0], preferred_element_type=jnp.float32)
        * score_scale
    )
    own_score = jnp.where(home_here[:, None, None], own_score, floor_value)
    local_top = jnp.maximum(request_top, own_score)
    weights = jnp.where(
        live_mask[:, None, None, :], jnp.exp(scores - local_top[owners][..., None]), 0.0
    )
    own_weight = jnp.where(home_here[:, None, None], jnp.exp(own_score - local_top), 0.0)
    block_sum = jnp.sum(weights, axis=-1)
    block_out = jnp.einsum(
        "bgjt,bgtd->bgjd",
        weights.astype(jnp.bfloat16),
        cache_kv[:, 1],
        preferred_element_type=jnp.float32,
    )
    onehot = members.astype(jnp.float32).T
    head_count = heads_here * per_group
    totals = jnp.dot(onehot, block_sum.reshape(local_blocks, head_count), precision=highest)
    totals = totals + own_weight.reshape(requests, head_count)
    own_part = own_weight.astype(jnp.bfloat16).astype(jnp.float32)[..., None] * fresh_kv[:, 1][
        :, :, None, :
    ].astype(jnp.float32)
    outputs = jnp.dot(
        onehot, block_out.reshape(local_blocks, head_count * head_dim), precision=highest
    )
    outputs = outputs + own_part.reshape(requests, head_count * head_dim)
    top_rows = local_top.reshape(requests, head_count)

    def combine(earlier, later):
        merged_top = jnp.maximum(earlier[0], later[0])
        left_scale = jnp.exp(earlier[0] - merged_top)
        right_scale = jnp.exp(later[0] - merged_top)
        return (
            merged_top,
            left_scale * earlier[1] + right_scale * later[1],
            left_scale[..., None] * earlier[2] + right_scale[..., None] * later[2],
        )

    merged = joined(
        (top_rows, totals, outputs.reshape(requests, head_count, head_dim)), "pool", combine
    )
    attended = (
        (merged[2] / merged[1][..., None])
        .astype(jnp.bfloat16)
        .reshape(requests, head_count * head_dim)
    )
    partial_value = jnp.dot(attended, out_weight, preferred_element_type=jnp.float32)
    return lax.psum_scatter(partial_value, "head", scatter_dimension=1, tiled=True)


def solution(mesh):
    return jax.shard_map(
        per_device,
        mesh=mesh,
        in_specs=(
            P("pool", "head"),
            P("pool", None, "head"),
            P("pool", None, "head", None, None),
            P("head", "pool"),
            P(),
            P(),
            P(),
            P(),
        ),
        out_specs=P(None, ("pool", "head")),
        check_vma=False,
    )
```

profile of v0, /device:TPU:1, one launch (start us, length us, event | category | flops | bytes accessed | tf_op | source)
XLA Modules:
  0.0 654.3 jit_solution(7553588376983548814)
XLA Ops:
  9.9 1.3 gather_fusion
  11.2 4.5 gather_fusion.1
  16.1 134.4 %all-gather.1 = bf16[64,1,2048]{2,1,0:T(2,128)(2,1)S(1)} all-gather(bf16[1,1,2048]{2,1,0:T(2,128)(2,1)S(1)} %bitcast.130), channel_id=1, replica_groups=mesh['pool'=64,'head'=4] {'pool'}, dimensions={0}, use_global_device_ids=true | all-gather | bytes 266240 | tf_op jit(solution)/shard_map/all_gather | solution.py:30
  153.5 2.3 fusion.44
  156.8 2.0 fusion.3
  160.9 130.7 %all-gather.2 = f32[64,32,16]{1,2,0:T(8,128)S(1)} all-gather(f32[1,32,16]{1,2,0:T(8,128)S(1)} %fusion.16), channel_id=2, replica_groups=mesh['pool'=64,'head'=4] {'pool'}, dimensions={0}, use_global_device_ids=true | all-gather | bytes 133120 | tf_op jit(solution)/shard_map/all_gather | solution.py:12
  291.6 133.1 %all_gather.16 = f32[64,32,16]{1,2,0:T(8,128)S(1)} all-gather(f32[1,32,16]{1,2,0:T(8,128)S(1)} %bitcast.127), channel_id=1, replica_groups=mesh['pool'=64,'head'=4] {'pool'}, dimensions={0}, use_global_device_ids=true | all-gather | bytes 133120 | tf_op jit(solution)/shard_map/all_gather | solution.py:12
  424.7 50.3 %all-gather.5.cloned.1.call-done = f32[64,32,16,128]{3,2,1,0:T(8,128)} async-done(((f32[1,32,16,128]{3,2,1,0:T(8,128)}), f32[64,32,16,128]{3,2,1,0:T(8,128)}) %all-gather.5.cloned.1.call-update) | async-done | bytes 16777232 | tf_op jit(solution)/shard_map/all_gather | solution.py:12
  476.0 11.6 %slice.65 = f32[63,32,16,128]{3,2,1,0:T(8,128)} slice(f32[64,32,16,128]{3,2,1,0:T(8,128)} %all-gather.5.cloned.1.call-done), slice={[1:64], [0:32], [0:16], [0:128]} | slice | bytes 33030144 | tf_op jit(solution)/shard_map/slice | solution.py:14
  487.6 89.1 %while.14 = (s32[]{:T(128)}, f32[32,16]{0,1:T(8,128)S(1)}, f32[32,16]{0,1:T(8,128)S(1)}, f32[32,16,128]{2,1,0:T(8,128)S(1)}, f32[63,32,16]{1,2,0:T(8,128)S(1)}, ...) while((s32[]{:T(128)}, f32[32,16]{0,1:T(8,128)S(1)}, f32[32,16]{0,1:T(8,128)S(1)}, ...), condition=%wide.region_6.7_spmd, body=%wide.region_5.6_spmd.sunk | while | flops 199682 | bytes 815205 | solution.py:15
  487.8 1.2 fusion.51
  489.2 1.2 fusion.51
  490.6 1.2 fusion.51
  492.0 1.2 fusion.51
  493.4 1.2 fusion.51
  494.8 1.2 fusion.51
  496.3 1.2 fusion.51
  497.7 1.2 fusion.51
  499.1 1.2 fusion.51
  500.5 1.2 fusion.51
  501.9 1.2 fusion.51
  503.3 1.2 fusion.51
  504.7 1.2 fusion.51
  506.2 1.2 fusion.51
  507.6 1.2 fusion.51
  509.0 1.2 fusion.51
  510.4 1.2 fusion.51
  511.8 1.2 fusion.51
  513.2 1.2 fusion.51
  514.7 1.2 fusion.51
  516.1 1.2 fusion.51
  517.5 1.2 fusion.51
  518.9 1.2 fusion.51
  520.3 1.2 fusion.51
  521.7 1.2 fusion.51
  523.1 1.2 fusion.51
  524.6 1.2 fusion.51
  526.0 1.2 fusion.51
  527.4 1.2 fusion.51
  528.8 1.2 fusion.51
  531.6 1.2 fusion.51
  533.0 1.2 fusion.51
  534.5 1.2 fusion.51
  535.9 1.2 fusion.51
  540.1 1.2 fusion.51
  541.5 1.2 fusion.51
  543.0 1.2 fusion.51
  544.4 1.2 fusion.51
  545.8 1.2 fusion.51
  550.0 1.2 fusion.51
  551.4 1.2 fusion.51
  552.9 1.2 fusion.51
  554.3 1.2 fusion.51
  558.5 1.2 fusion.51
  559.9 1.2 fusion.51
  561.4 1.2 fusion.51
  562.8 1.2 fusion.51
  567.0 1.2 fusion.51
  568.4 1.2 fusion.51
  569.8 1.2 fusion.51
  571.3 1.2 fusion.51
  572.7 1.2 fusion.51
  578.0 68.1 %reduce-scatter.4.cloned.1.call-done = f32[32,32]{1,0:T(8,128)} async-done(((f32[128,32]{1,0:T(8,128)}), f32[32,32]{1,0:T(8,128)}) %reduce-scatter.4.cloned.1.call-update) | async-done | bytes 4112
  646.1 1.4 copy.57
  (263 shorter events, 35.9 us)
Async XLA Ops:
  6.5 570.4 %copy-start = (bf16[2048,128]{1,0:T(8,128)(2,1)S(1)}, bf16[2048,128]{1,0:T(8,128)(2,1)}, u32[]{:S(2)}) copy-start(bf16[2048,128]{1,0:T(8,128)(2,1)} %param.13) | copy-start | bytes 1572868
  6.5 4.7 copy-start.1
  6.5 468.5 %all-gather.5.cloned.1.call-start = ((), (), s32[]{:S(2)}) async-start(), calls=%async_computation.1 | async-start | bytes 17039360 | tf_op jit(solution)/shard_map/all_gather | solution.py:12
  11.2 4.8 copy-start.4
  11.2 4.9 copy-start.3
  11.2 140.1 %copy-start.2 = (s32[32]{0:T(128)S(1)}, s32[32]{0:T(128)}, u32[]{:S(2)}) copy-start(s32[32]{0:T(128)} %param.17) | copy-start | bytes 388
  160.2 485.9 %reduce-scatter.4.cloned.1.call-start = ((), (), s32[]{:S(2)}) async-start(), calls=%async_computation.2 | async-start | bytes 81920
Sparse Core Ops, SparseCore 0:
  160.3 314.6 all-gather.4
  578.1 67.9 reduce-scatter.3
where the time goes:
time: 657 us; the launch traced here: 654 us
  blocking collectives  398 us (61%)
  waiting for transfers between devices  118 us (18%)
  other arithmetic  81.6 us (12%)
  local copies, waits for them, and re-layouts  34.7 us (5%)
  between operations  13.6 us (2%)
    all_gather x2, blocking collectives, joined(): pieces = jax.tree.map(lambda part: lax.all_gather(part, axis), value)  264 us
    all_gather x1, blocking collectives, per_device(): every_slot = lax.all_gather(queries, 'pool', axis=0, tiled=True)  134 us
    add x63, other arithmetic, combine(): left_scale[..., None] * earlier[2] + right_scale[..., None] * later[2]  76.8 us
    unnamed x3, waiting for transfers between devices  68.1 us
    all_gather x1, waiting for transfers between devices, joined(): pieces = jax.tree.map(lambda part: lax.all_gather(part, axis), value)  50.3 us
  transfers between devices with their start and end apart: 2, of which 2 were waited for; matrix products, arithmetic and copies ran while one was open for 0% of the time, Pallas kernels for 0%

commit v1 on v0

v1 whole, which is shorter than its diff:
```python
import functools
import itertools
import math

import jax
import jax.numpy as jnp
from jax import lax
from jax.experimental import pallas as pl
from jax.experimental.pallas import tpu as pltpu
from jax.sharding import PartitionSpec as P

MESH = pl.DeviceIdType.MESH
LOW = -1e30
POOL = 64
HEADS = 4
Z, X = 8, 4
BLOCKS_HERE = 16
BLK = 256
HD = 128
REQ = 32
MAXB = 32
QH_HERE = 16
COMB = 32


def pool_offsets():
    steps = []
    for yl, z, x in itertools.product(range(2), range(Z), range(X)):
        hops = yl + min(z, Z - z) + min(x, X - x)
        if hops:
            steps.append((-hops, yl, z, x))
    return [step[1:] for step in sorted(steps)]


OFFSETS = pool_offsets()


def shifted(p, step):
    yl, z, x = p // 32, (p // X) % Z, p % X
    return ((yl + step[0]) % 2) * 32 + ((z + step[1]) % Z) * X + (x + step[2]) % X


def kernel(
    q_ref,
    new_ref,
    tab_v,
    tab_s,
    home_s,
    cnt_s,
    len_s,
    cache_hbm,
    w_hbm,
    out_ref,
    cache,
    weight,
    q_all,
    q_mine,
    scores,
    o_stack,
    o_send,
    o_recv,
    st_send,
    st_recv,
    st_turn,
    att_mine,
    att,
    y_all,
    load_sem,
    q_sem,
    p_sem,
    s_sem,
    a_sem,
    y_sem,
):
    p = lax.axis_index("pool")
    h = lax.axis_index("head")
    yl, z, x = p // 32, (p // X) % Z, p % X
    core = h % 2
    is_comb = (yl + z + x) % 2 == core
    mine = p // 2

    barrier = pltpu.get_barrier_semaphore()
    for step in OFFSETS:
        pl.semaphore_signal(
            barrier, inc=1, device_id=(shifted(p, step), h), device_id_type=MESH
        )
    for i in range(1, HEADS):
        pl.semaphore_signal(
            barrier, inc=1, device_id=(p, (h + i) % HEADS), device_id_type=MESH
        )
    loads = [
        pltpu.make_async_copy(cache_hbm.at[b], cache.at[b], load_sem.at[0])
        for b in range(BLOCKS_HERE)
    ]
    for load in loads:
        load.start()
    w_load = pltpu.make_async_copy(w_hbm, weight, load_sem.at[1])
    w_load.start()

    q_row = q_ref[...].astype(jnp.float32)
    q_rows = jnp.concatenate(
        [q_row[:, i * HD : (i + 1) * HD] for i in range(QH_HERE)], axis=0
    )
    q_mine[...] = q_rows.astype(jnp.bfloat16)
    pl.semaphore_wait(barrier, POOL - 1 + HEADS - 1)

    for step in OFFSETS:
        pltpu.make_async_remote_copy(
            q_mine,
            q_all.at[p],
            q_sem.at[0],
            q_sem.at[1],
            device_id=(shifted(p, step), h),
            device_id_type=MESH,
        ).start()
    pltpu.make_async_copy(q_mine, q_all.at[p], q_sem.at[1]).start()

    table = tab_v[...]
    entry = lax.broadcasted_iota(jnp.int32, (REQ, MAXB), 0) * MAXB + lax.broadcasted_iota(
        jnp.int32, (REQ, MAXB), 1
    )
    places = [
        jnp.max(jnp.where(table == p * BLOCKS_HERE + b, entry, 0))
        for b in range(BLOCKS_HERE)
    ]
    owners = [place >> 5 for place in places]
    ranks = [place & 31 for place in places]

    def add_counts(i, starts):
        return tuple(
            start + jnp.where(i < rank, cnt_s[tab_s[owner, i]], 0)
            for start, owner, rank in zip(starts, owners, ranks)
        )

    starts = lax.fori_loop(
        0, MAXB - 1, add_counts, tuple(jnp.int32(0) for _ in range(BLOCKS_HERE))
    )
    live = [
        jnp.minimum(cnt_s[p * BLOCKS_HERE + b], len_s[owners[b]] - starts[b])
        for b in range(BLOCKS_HERE)
    ]
    slots = [home_s[owner] for owner in owners]

    def find_own(r, found):
        return jnp.where(home_s[r] == p, r, found)

    own = lax.fori_loop(0, REQ, find_own, jnp.int32(2 * HD))

    scale = 1.0 / math.sqrt(HD)
    upper = lax.broadcasted_iota(jnp.int32, (QH_HERE, HD), 0) < 8
    new_kv = new_ref[0].astype(jnp.float32)
    new_k = jnp.where(upper, new_kv[0:1, :HD], new_kv[0:1, HD:])
    new_v = jnp.where(upper, new_kv[1:2, :HD], new_kv[1:2, HD:])
    own_score = jnp.sum(q_rows * new_k, axis=1, keepdims=True) * scale
    lane = lax.broadcasted_iota(jnp.int32, (QH_HERE, HD), 1)
    tops = jnp.where(lane == own, own_score, LOW)

    for load in loads:
        load.wait()
    whole = pltpu.make_async_copy(q_all, q_all, q_sem.at[1])
    whole.wait()
    token = lax.broadcasted_iota(jnp.int32, (QH_HERE, BLK), 1)
    for b in range(BLOCKS_HERE):
        q = q_all[slots[b]].astype(jnp.float32)
        wide = jnp.concatenate(
            [jnp.where(upper, q, 0.0), jnp.where(upper, 0.0, q)], axis=1
        ).astype(jnp.bfloat16)
        keys = jnp.concatenate([cache[b, 0, 0], cache[b, 0, 1]], axis=1)
        s = lax.dot_general(
            wide, keys, (((1,), (1,)), ((), ())), preferred_element_type=jnp.float32
        )
        s = jnp.where(token < live[b], s * scale, LOW)
        scores[b] = s
        top = jnp.max(s, axis=1, keepdims=True)
        tops = jnp.where(lane == owners[b], jnp.maximum(tops, top), tops)

    own_top = jnp.max(jnp.where(lane == own, tops, LOW), axis=1, keepdims=True)
    own_weight = jnp.exp(own_score - own_top)
    totals = jnp.where(lane == own, own_weight, 0.0)
    for b in range(BLOCKS_HERE):
        top = jnp.max(jnp.where(lane == owners[b], tops, LOW), axis=1, keepdims=True)
        weights = jnp.where(token < live[b], jnp.exp(scores[b] - top), 0.0)
        total = jnp.sum(weights, axis=1, keepdims=True)
        totals = jnp.where(lane == owners[b], totals + total, totals)
        values = jnp.concatenate([cache[b, 1, 0], cache[b, 1, 1]], axis=1)
        o = jnp.dot(
            weights.astype(jnp.bfloat16), values, preferred_element_type=jnp.float32
        )
        o = jnp.concatenate([o[:8, :HD], o[8:, HD:]], axis=0)
        o_stack[b * QH_HERE : (b + 1) * QH_HERE, :] = o.astype(jnp.bfloat16)

    stats = jnp.where(lane < REQ, totals, pltpu.roll(tops, REQ, 1))
    for i in range(QH_HERE):
        st_send[i] = stats[i : i + 1, :]

    column = lax.broadcasted_iota(jnp.int32, (1, BLOCKS_HERE * QH_HERE), 1)
    goal = jnp.zeros((1, BLOCKS_HERE * QH_HERE), jnp.int32)
    for b in range(BLOCKS_HERE):
        goal = jnp.where(column // QH_HERE == b, owners[b], goal)
    goal = goal + (column % QH_HERE) * REQ
    row = lax.broadcasted_iota(jnp.int32, (QH_HERE * REQ, BLOCKS_HERE * QH_HERE), 0)
    pick = jnp.where(row == goal, 1.0, 0.0).astype(jnp.bfloat16)
    merged = jnp.dot(pick, o_stack[...], preferred_element_type=jnp.float32)
    own_part = own_weight.astype(jnp.bfloat16).astype(jnp.float32) * new_v
    request = lax.broadcasted_iota(jnp.int32, (REQ, HD), 0)
    for i in range(QH_HERE):
        part = merged[i * REQ : (i + 1) * REQ, :]
        part = part + jnp.where(request == own, own_part[i : i + 1, :], 0.0)
        o_send[2 * i] = part[:16].astype(jnp.bfloat16)
        o_send[2 * i + 1] = part[16:].astype(jnp.bfloat16)

    for i in range(COMB):
        k = (mine + i + COMB // 2) % COMB
        to = 2 * k + (k // 16 + (k // 2) % Z + core) % 2

        def send(k=k, to=to):
            pltpu.make_async_remote_copy(
                st_send.at[k // 2],
                st_recv.at[p],
                s_sem.at[0],
                s_sem.at[1],
                device_id=(to, h),
                device_id_type=MESH,
            ).start()
            pltpu.make_async_remote_copy(
                o_send.at[k],
                o_recv.at[p],
                p_sem.at[0],
                p_sem.at[1],
                device_id=(to, h),
                device_id_type=MESH,
            ).start()

        if i == COMB // 2:

            @pl.when(is_comb)
            def _():
                pltpu.make_async_copy(
                    st_send.at[k // 2], st_recv.at[p], s_sem.at[1]
                ).start()
                pltpu.make_async_copy(o_send.at[k], o_recv.at[p], p_sem.at[1]).start()

            pl.when(jnp.logical_not(is_comb))(send)
        else:
            send()

    half = mine % 2

    @pl.when(is_comb)
    def _():
        pltpu.make_async_copy(st_recv, st_recv, s_sem.at[1]).wait()
        st_turn[...] = jnp.transpose(st_recv[:, 0, :])
        tot = st_turn[pl.ds(pl.multiple_of(half * 16, 16), 16), :]
        top = st_turn[pl.ds(pl.multiple_of(REQ + half * 16, 16), 16), :]
        top = jnp.where(tot > 0.0, top, LOW)
        most = jnp.max(top, axis=1, keepdims=True)
        factor = jnp.where(tot > 0.0, jnp.exp(top - most), 0.0)
        factor = factor / jnp.sum(factor * tot, axis=1, keepdims=True)
        pltpu.make_async_copy(o_recv, o_recv, p_sem.at[1]).wait()
        sums = [jnp.zeros((16, HD), jnp.float32) for _ in range(4)]
        for i in range(POOL):
            sums[i % 4] = sums[i % 4] + factor[:, i : i + 1] * o_recv[i].astype(
                jnp.float32
            )
        att_mine[...] = ((sums[0] + sums[1]) + (sums[2] + sums[3])).astype(jnp.bfloat16)
        for step in OFFSETS:
            pltpu.make_async_remote_copy(
                att_mine,
                att.at[mine],
                a_sem.at[0],
                a_sem.at[1],
                device_id=(shifted(p, step), h),
                device_id_type=MESH,
            ).start()
        pltpu.make_async_copy(att_mine, att.at[mine], a_sem.at[1]).start()

    w_load.wait()
    pltpu.make_async_copy(att, att, a_sem.at[1]).wait()
    wide = jnp.concatenate(
        [
            jnp.concatenate([att[2 * i], att[2 * i + 1]], axis=0)
            for i in range(QH_HERE)
        ],
        axis=1,
    )
    y_all[h] = jnp.dot(wide, weight[...], preferred_element_type=jnp.float32)
    y_copies = []
    for i in range(1, HEADS):
        copy = pltpu.make_async_remote_copy(
            y_all.at[h],
            y_all.at[h],
            y_sem.at[0],
            y_sem.at[1],
            device_id=(p, (h + i) % HEADS),
            device_id_type=MESH,
        )
        copy.start()
        y_copies.append(copy)
    three = y_all.at[pl.ds(0, HEADS - 1)]
    pltpu.make_async_copy(three, three, y_sem.at[1]).wait()
    y = (y_all[0] + y_all[1]) + (y_all[2] + y_all[3])
    part = y[:, :32]
    for i in range(1, HEADS):
        part = jnp.where(h == i, y[:, i * 32 : (i + 1) * 32], part)
    out_ref[...] = part

    pltpu.make_async_copy(three, three, y_sem.at[0]).wait()
    others = q_all.at[pl.ds(0, POOL - 1)]
    pltpu.make_async_copy(others, others, q_sem.at[0]).wait()

    @pl.when(is_comb)
    def _():
        most_o = o_send.at[pl.ds(0, COMB - 1)]
        pltpu.make_async_copy(most_o, most_o, p_sem.at[0]).wait()
        most_s = st_recv.at[pl.ds(0, COMB - 1)]
        pltpu.make_async_copy(most_s, most_s, s_sem.at[0]).wait()
        pltpu.make_async_copy(others, others, a_sem.at[0]).wait()

    @pl.when(jnp.logical_not(is_comb))
    def _():
        pltpu.make_async_copy(o_send, o_send, p_sem.at[0]).wait()
        all_s = st_recv.at[pl.ds(0, COMB)]
        pltpu.make_async_copy(all_s, all_s, s_sem.at[0]).wait()


def per_device(
    queries, new_kv, cache_kv, out_weight, block_table, home_slot, block_counts, lengths
):
    vmem = pl.BlockSpec(memory_space=pltpu.VMEM)
    smem = pl.BlockSpec(memory_space=pltpu.SMEM)
    hbm = pl.BlockSpec(memory_space=pltpu.HBM)
    bf16, f32 = jnp.bfloat16, jnp.float32
    dma = pltpu.SemaphoreType.DMA((2,))
    return pl.pallas_call(
        kernel,
        out_shape=jax.ShapeDtypeStruct((REQ, 32), f32),
        in_specs=[vmem, vmem, vmem, smem, smem, smem, smem, hbm, hbm],
        out_specs=vmem,
        scratch_shapes=[
            pltpu.VMEM((BLOCKS_HERE, 2, 2, BLK, HD), bf16),
            pltpu.VMEM((QH_HERE * HD, HD), bf16),
            pltpu.VMEM((POOL, QH_HERE, HD), bf16),
            pltpu.VMEM((QH_HERE, HD), bf16),
            pltpu.VMEM((BLOCKS_HERE, QH_HERE, BLK), f32),
            pltpu.VMEM((BLOCKS_HERE * QH_HERE, HD), bf16),
            pltpu.VMEM((COMB, 16, HD), bf16),
            pltpu.VMEM((POOL, 16, HD), bf16),
            pltpu.VMEM((QH_HERE, 1, HD), f32),
            pltpu.VMEM((POOL, 1, HD), f32),
            pltpu.VMEM((HD, POOL), f32),
            pltpu.VMEM((16, HD), bf16),
            pltpu.VMEM((COMB, 16, HD), bf16),
            pltpu.VMEM((HEADS, REQ, HD), f32),
            dma,
            dma,
            dma,
            dma,
            dma,
            dma,
        ],
        compiler_params=pltpu.CompilerParams(
            collective_id=0, has_side_effects=True, vmem_limit_bytes=62 * 1024 * 1024
        ),
        name="decode",
    )(
        queries,
        new_kv,
        block_table,
        block_table,
        home_slot,
        block_counts,
        lengths,
        cache_kv,
        out_weight,
    )


def solution(mesh):
    return jax.shard_map(
        per_device,
        mesh=mesh,
        in_specs=(
            P("pool", "head"),
            P("pool", None, "head"),
            P("pool", None, "head", None, None),
            P("head", "pool"),
            P(),
            P(),
            P(),
            P(),
        ),
        out_specs=P(None, ("pool", "head")),
        check_vma=False,
    )
```

time: 657 us -> 43.2 us (0.07)
  blocking collectives: 398 us -> 0 us
  waiting for transfers between devices: 118 us -> 0 us
  other arithmetic: 81.6 us -> 0 us
  Pallas kernels: 0 us -> 41.6 us
  local copies, waits for them, and re-layouts: 34.7 us -> 1.32 us
  between operations: 13.6 us -> 0.01 us
    all_gather x3 -> x0, blocking collectives: 398 us -> none  [the longest x2 264 us: joined(): pieces = jax.tree.map(lambda part: lax.all_gather(part, axis), value)]
    add x127 -> x0, other arithmetic: 78.1 us -> none  [the longest x63 76.8 us: combine(): left_scale[..., None] * earlier[2] + right_scale[..., None] * later[2]]
    unnamed x3 -> x0, waiting for transfers between devices: 68.1 us -> none
    all_gather x1 -> x0, waiting for transfers between devices: 50.3 us -> none  [joined(): pieces = jax.tree.map(lambda part: lax.all_gather(part, axis), value)]
    pallas_call x0 -> x1, Pallas kernels: none -> 41.6 us  [per_device(): pl.pallas_call(kernel, out_shape=jax.ShapeDtypeStruct((REQ, 32), f32), in...]
    slice x4 -> x0, local copies, waits for them, and re-layouts: 11.7 us -> none  [the longest x3 11.7 us: joined(): tail = jax.tree.map(lambda part: part[1:], pieces)]
    exp x126 -> x0, local copies, waits for them, and re-layouts: 9.35 us -> none  [the longest x63 4.71 us: combine(): right_scale = jnp.exp(later[0] - merged_top)]
    gather x9 -> x0, local copies, waits for them, and re-layouts: 9.1 us -> none  [the longest x2 4.6 us: per_device(): listed = block_counts[block_table]]
  transfers between devices with their start and end apart: 2 -> 0, of which waited for: 2 -> 0; matrix products, arithmetic and copies ran while one was open for 0% -> 0% of each run, Pallas kernels for 0% -> 0%
where the time goes in v1:
time: 43.2 us; the launch traced here: 42.9 us
  Pallas kernels  41.6 us (96%)
  local copies, waits for them, and re-layouts  1.32 us (3%)
    pallas_call x1, Pallas kernels, per_device(): pl.pallas_call(kernel, out_shape=jax.ShapeDtypeStruct((REQ, 32), f32), in...  41.6 us
    unnamed x1, local copies, waits for them, and re-layouts  1.32 us

profile of v1, /device:TPU:1, one launch (start us, length us, event | category | flops | bytes accessed | tf_op | source)
XLA Modules:
  0.0 42.9 jit_solution(6685288045578923264)
XLA Ops:
  0.0 41.6 %decode.1 = f32[32,32]{1,0:T(8,128)} custom-call(bf16[1,2048]{1,0:T(2,128)(2,1)} %q_ref.1, bf16[1,2,256]{2,1,0:T(2,128)(2,1)} %new_ref.1, s32[32,32]{1,0:T(8,128)} %tab_s.1, s32[32,32]{1,0:T(8,128)} %tab_s.1, s32[32]{0:T(128)} %home_s.1, s32[1024]{0:T(1024)} %cnt_s.1, s32[32]{0:T(128)} %len_s.1, bf16[16,2,2,256,128]{4,3,2,1,0:T(8,128)(2,1)} %cache_hbm.1, ...), custom_call_target="tpu_custom_call" | custom-call | tf_op jit(solution)/shard_map/decode/pallas_call | solution.py:334
  41.6 1.3 %copy.10 = f32[32,32]{1,0:T(8,128)} copy(f32[32,32]{1,0:T(8,128)} %decode.1) | data formatting | bytes 8192

commit v2 on v1

--- a/solution.py
+++ b/solution.py
@@ -41,6 +41,15 @@
 
 
 def kernel(
+    q_hbm,
+    new_hbm,
+    tab_hbm,
+    home_hbm,
+    cnt_hbm,
+    len_hbm,
+    cache_hbm,
+    w_hbm,
+    out_ref,
     q_ref,
     new_ref,
     tab_v,
@@ -48,9 +57,6 @@
     home_s,
     cnt_s,
     len_s,
-    cache_hbm,
-    w_hbm,
-    out_ref,
     cache,
     weight,
     q_all,
@@ -64,7 +70,8 @@
     st_turn,
     att_mine,
     att,
-    y_all,
+    y_send,
+    y_recv,
     load_sem,
     q_sem,
     p_sem,
@@ -88,6 +95,23 @@
         pl.semaphore_signal(
             barrier, inc=1, device_id=(p, (h + i) % HEADS), device_id_type=MESH
         )
+    q_load = pltpu.make_async_copy(q_hbm, q_ref, load_sem.at[2])
+    q_load.start()
+    small_loads = [
+        pltpu.make_async_copy(source, target, load_sem.at[3 + i])
+        for i, (source, target) in enumerate(
+            (
+                (tab_hbm, tab_v),
+                (tab_hbm, tab_s),
+                (cnt_hbm, cnt_s),
+                (home_hbm, home_s),
+                (len_hbm, len_s),
+                (new_hbm, new_ref),
+            )
+        )
+    ]
+    for load in small_loads:
+        load.start()
     loads = [
         pltpu.make_async_copy(cache_hbm.at[b], cache.at[b], load_sem.at[0])
         for b in range(BLOCKS_HERE)
@@ -97,6 +121,7 @@
     w_load = pltpu.make_async_copy(w_hbm, weight, load_sem.at[1])
     w_load.start()
 
+    q_load.wait()
     q_row = q_ref[...].astype(jnp.float32)
     q_rows = jnp.concatenate(
         [q_row[:, i * HD : (i + 1) * HD] for i in range(QH_HERE)], axis=0
@@ -115,6 +140,8 @@
         ).start()
     pltpu.make_async_copy(q_mine, q_all.at[p], q_sem.at[1]).start()
 
+    for load in small_loads:
+        load.wait()
     table = tab_v[...]
     entry = lax.broadcasted_iota(jnp.int32, (REQ, MAXB), 0) * MAXB + lax.broadcasted_iota(
         jnp.int32, (REQ, MAXB), 1
@@ -283,27 +310,27 @@
         ],
         axis=1,
     )
-    y_all[h] = jnp.dot(wide, weight[...], preferred_element_type=jnp.float32)
-    y_copies = []
+    y = jnp.dot(wide, weight[...], preferred_element_type=jnp.float32)
+    for i in range(HEADS):
+        y_send[i] = jnp.concatenate(
+            [y[8 * j : 8 * j + 8, 32 * i : 32 * i + 32] for j in range(4)], axis=1
+        )
     for i in range(1, HEADS):
-        copy = pltpu.make_async_remote_copy(
-            y_all.at[h],
-            y_all.at[h],
+        pltpu.make_async_remote_copy(
+            y_send.at[(h + i) % HEADS],
+            y_recv.at[h],
             y_sem.at[0],
             y_sem.at[1],
             device_id=(p, (h + i) % HEADS),
             device_id_type=MESH,
-        )
-        copy.start()
-        y_copies.append(copy)
-    three = y_all.at[pl.ds(0, HEADS - 1)]
-    pltpu.make_async_copy(three, three, y_sem.at[1]).wait()
-    y = (y_all[0] + y_all[1]) + (y_all[2] + y_all[3])
-    part = y[:, :32]
-    for i in range(1, HEADS):
-        part = jnp.where(h == i, y[:, i * 32 : (i + 1) * 32], part)
-    out_ref[...] = part
-
+        ).start()
+    pltpu.make_async_copy(y_send.at[h], y_recv.at[h], y_sem.at[1]).start()
+    pltpu.make_async_copy(y_recv, y_recv, y_sem.at[1]).wait()
+    y = (y_recv[0] + y_recv[1]) + (y_recv[2] + y_recv[3])
+    for j in range(4):
+        out_ref[8 * j : 8 * j + 8, :] = y[:, 32 * j : 32 * j + 32]
+
+    three = y_send.at[pl.ds(0, HEADS - 1)]
     pltpu.make_async_copy(three, three, y_sem.at[0]).wait()
     others = q_all.at[pl.ds(0, POOL - 1)]
     pltpu.make_async_copy(others, others, q_sem.at[0]).wait()
@@ -327,16 +354,22 @@
     queries, new_kv, cache_kv, out_weight, block_table, home_slot, block_counts, lengths
 ):
     vmem = pl.BlockSpec(memory_space=pltpu.VMEM)
-    smem = pl.BlockSpec(memory_space=pltpu.SMEM)
     hbm = pl.BlockSpec(memory_space=pltpu.HBM)
     bf16, f32 = jnp.bfloat16, jnp.float32
     dma = pltpu.SemaphoreType.DMA((2,))
     return pl.pallas_call(
         kernel,
-        out_shape=jax.ShapeDtypeStruct((REQ, 32), f32),
-        in_specs=[vmem, vmem, vmem, smem, smem, smem, smem, hbm, hbm],
+        out_shape=pltpu.VMEM((REQ, 32), f32),
+        in_specs=[hbm] * 8,
         out_specs=vmem,
         scratch_shapes=[
+            pltpu.VMEM(queries.shape, bf16),
+            pltpu.VMEM(new_kv.shape, bf16),
+            pltpu.VMEM(block_table.shape, jnp.int32),
+            pltpu.SMEM(block_table.shape, jnp.int32),
+            pltpu.SMEM(home_slot.shape, jnp.int32),
+            pltpu.SMEM(block_counts.shape, jnp.int32),
+            pltpu.SMEM(lengths.shape, jnp.int32),
             pltpu.VMEM((BLOCKS_HERE, 2, 2, BLK, HD), bf16),
             pltpu.VMEM((QH_HERE * HD, HD), bf16),
             pltpu.VMEM((POOL, QH_HERE, HD), bf16),
@@ -350,8 +383,9 @@
             pltpu.VMEM((HD, POOL), f32),
             pltpu.VMEM((16, HD), bf16),
             pltpu.VMEM((COMB, 16, HD), bf16),
-            pltpu.VMEM((HEADS, REQ, HD), f32),
-            dma,
+            pltpu.VMEM((HEADS, 8, HD), f32),
+            pltpu.VMEM((HEADS, 8, HD), f32),
+            pltpu.SemaphoreType.DMA((9,)),
             dma,
             dma,
             dma,
@@ -365,7 +399,6 @@
     )(
         queries,
         new_kv,
-        block_table,
         block_table,
         home_slot,
         block_counts,

time: 43.2 us -> 40.6 us (0.940)
  Pallas kernels: 41.6 us -> 39.8 us
  local copies, waits for them, and re-layouts: 1.32 us -> 0.61 us
    pallas_call x1, Pallas kernels: 41.6 us -> 39.8 us  [per_device(): pl.pallas_call(kernel, out_shape=pltpu.VMEM((REQ, 32), f32), in_specs=[hb...]
    unnamed x1, local copies, waits for them, and re-layouts: 1.32 us -> 0.61 us
where the time goes in v2:
time: 40.6 us; the launch traced here: 40.4 us
  Pallas kernels  39.8 us (98%)
  local copies, waits for them, and re-layouts  0.61 us (2%)
    pallas_call x1, Pallas kernels, per_device(): pl.pallas_call(kernel, out_shape=pltpu.VMEM((REQ, 32), f32), in_specs=[hb...  39.8 us

profile of v2, /device:TPU:1, one launch (start us, length us, event | category | flops | bytes accessed | tf_op | source)
XLA Modules:
  0.0 40.4 jit_solution(5541720123906314586)
XLA Ops:
  0.0 39.8 %decode.1 = f32[32,32]{1,0:T(8,128)S(1)} custom-call(bf16[1,2048]{1,0:T(2,128)(2,1)} %q_hbm.1, bf16[1,2,256]{2,1,0:T(2,128)(2,1)} %new_hbm.1, s32[32,32]{1,0:T(8,128)} %tab_hbm.1, s32[32]{0:T(128)} %home_hbm.1, s32[1024]{0:T(1024)} %cnt_hbm.1, s32[32]{0:T(128)} %len_hbm.1, bf16[16,2,2,256,128]{4,3,2,1,0:T(8,128)(2,1)} %cache_hbm.1, bf16[2048,128]{1,0:T(8,128)(2,1)} %w_hbm.1), custom_call_target="tpu_custom_call" | custom-call | tf_op jit(solution)/shard_map/decode/pallas_call | solution.py:360
  39.8 0.6 %copy.10 = f32[32,32]{1,0:T(8,128)} copy(f32[32,32]{1,0:T(8,128)S(1)} %decode.1) | data formatting | bytes 8192

commit v3 on v2

--- a/solution.py
+++ b/solution.py
@@ -33,6 +33,8 @@
 
 
 OFFSETS = pool_offsets()
+RELAYED = (2, Z - 2)
+ROW = {step: row for row, step in enumerate((2, 6, 0, 1, 3, 4, 5, 7))}
 
 
 def shifted(p, step):
@@ -62,6 +64,7 @@
     q_all,
     q_mine,
     scores,
+    turned,
     o_stack,
     o_send,
     o_recv,
@@ -129,16 +132,41 @@
     q_mine[...] = q_rows.astype(jnp.bfloat16)
     pl.semaphore_wait(barrier, POOL - 1 + HEADS - 1)
 
-    for step in OFFSETS:
+    column = yl * X + x
+    for along in RELAYED:
         pltpu.make_async_remote_copy(
             q_mine,
-            q_all.at[p],
+            q_all.at[column * Z + ROW[Z - along]],
             q_sem.at[0],
-            q_sem.at[1],
-            device_id=(shifted(p, step), h),
+            q_sem.at[2],
+            device_id=(shifted(p, (0, along, 0)), h),
             device_id_type=MESH,
         ).start()
-    pltpu.make_async_copy(q_mine, q_all.at[p], q_sem.at[1]).start()
+    for step in OFFSETS:
+        if step[1] not in RELAYED:
+            pltpu.make_async_remote_copy(
+                q_mine,
+                q_all.at[column * Z + ROW[(Z - step[1]) % Z]],
+                q_sem.at[0],
+                q_sem.at[1],
+                device_id=(shifted(p, step), h),
+                device_id_type=MESH,
+            ).start()
+    pltpu.make_async_copy(
+        q_mine, q_all.at[column * Z + ROW[0]], q_sem.at[1]
+    ).start()
+    two = q_all.at[pl.ds(column * Z, 2)]
+    pltpu.make_async_copy(two, two, q_sem.at[2]).wait()
+    for step in OFFSETS:
+        if step[1] == 0:
+            pltpu.make_async_remote_copy(
+                two,
+                two,
+                q_sem.at[0],
+                q_sem.at[1],
+                device_id=(shifted(p, step), h),
+                device_id_type=MESH,
+            ).start()
 
     for load in small_loads:
         load.wait()
@@ -166,7 +194,14 @@
         jnp.minimum(cnt_s[p * BLOCKS_HERE + b], len_s[owners[b]] - starts[b])
         for b in range(BLOCKS_HERE)
     ]
-    slots = [home_s[owner] for owner in owners]
+    slots = []
+    for owner in owners:
+        slot = home_s[owner]
+        away = ((slot >> 2) - z) & (Z - 1)
+        row = jnp.int32(0)
+        for step, place in ROW.items():
+            row = jnp.where(away == step, place, row)
+        slots.append(((slot >> 5) * X + (slot & (X - 1))) * Z + row)
 
     def find_own(r, found):
         return jnp.where(home_s[r] == p, r, found)
@@ -184,18 +219,19 @@
 
     for load in loads:
         load.wait()
-    whole = pltpu.make_async_copy(q_all, q_all, q_sem.at[1])
+    for b in range(BLOCKS_HERE):
+        for i in range(2):
+            turned[b, i * HD : (i + 1) * HD, :] = jnp.transpose(cache[b, 0, i])
+    most = q_all.at[pl.ds(0, POOL - 2)]
+    whole = pltpu.make_async_copy(most, most, q_sem.at[1])
     whole.wait()
     token = lax.broadcasted_iota(jnp.int32, (QH_HERE, BLK), 1)
+    first = jnp.where(upper, 1.0, 0.0).astype(jnp.bfloat16)
+    second = jnp.where(upper, 0.0, 1.0).astype(jnp.bfloat16)
     for b in range(BLOCKS_HERE):
-        q = q_all[slots[b]].astype(jnp.float32)
-        wide = jnp.concatenate(
-            [jnp.where(upper, q, 0.0), jnp.where(upper, 0.0, q)], axis=1
-        ).astype(jnp.bfloat16)
-        keys = jnp.concatenate([cache[b, 0, 0], cache[b, 0, 1]], axis=1)
-        s = lax.dot_general(
-            wide, keys, (((1,), (1,)), ((), ())), preferred_element_type=jnp.float32
-        )
+        q = q_all[slots[b]]
+        wide = jnp.concatenate([q * first, q * second], axis=1)
+        s = jnp.dot(wide, turned[b], preferred_element_type=jnp.float32)
         s = jnp.where(token < live[b], s * scale, LOW)
         scores[b] = s
         top = jnp.max(s, axis=1, keepdims=True)
@@ -236,40 +272,37 @@
         o_send[2 * i] = part[:16].astype(jnp.bfloat16)
         o_send[2 * i + 1] = part[16:].astype(jnp.bfloat16)
 
-    for i in range(COMB):
-        k = (mine + i + COMB // 2) % COMB
-        to = 2 * k + (k // 16 + (k // 2) % Z + core) % 2
-
-        def send(k=k, to=to):
-            pltpu.make_async_remote_copy(
-                st_send.at[k // 2],
-                st_recv.at[p],
-                s_sem.at[0],
-                s_sem.at[1],
-                device_id=(to, h),
-                device_id_type=MESH,
-            ).start()
-            pltpu.make_async_remote_copy(
-                o_send.at[k],
-                o_recv.at[p],
-                p_sem.at[0],
-                p_sem.at[1],
-                device_id=(to, h),
-                device_id_type=MESH,
-            ).start()
-
-        if i == COMB // 2:
-
-            @pl.when(is_comb)
-            def _():
-                pltpu.make_async_copy(
-                    st_send.at[k // 2], st_recv.at[p], s_sem.at[1]
+    def send_partials(parity):
+        for step in OFFSETS:
+            if sum(step) % 2 == parity:
+                to = shifted(p, step)
+                k = to // 2
+                pltpu.make_async_remote_copy(
+                    st_send.at[k // 2],
+                    st_recv.at[p],
+                    s_sem.at[0],
+                    s_sem.at[1],
+                    device_id=(to, h),
+                    device_id_type=MESH,
                 ).start()
-                pltpu.make_async_copy(o_send.at[k], o_recv.at[p], p_sem.at[1]).start()
-
-            pl.when(jnp.logical_not(is_comb))(send)
-        else:
-            send()
+                pltpu.make_async_remote_copy(
+                    o_send.at[k],
+                    o_recv.at[p],
+                    p_sem.at[0],
+                    p_sem.at[1],
+                    device_id=(to, h),
+                    device_id_type=MESH,
+                ).start()
+
+    @pl.when(is_comb)
+    def _():
+        send_partials(0)
+        pltpu.make_async_copy(st_send.at[mine // 2], st_recv.at[p], s_sem.at[1]).start()
+        pltpu.make_async_copy(o_send.at[mine], o_recv.at[p], p_sem.at[1]).start()
+
+    @pl.when(jnp.logical_not(is_comb))
+    def _():
+        send_partials(1)
 
     half = mine % 2
 
@@ -375,6 +408,7 @@
             pltpu.VMEM((POOL, QH_HERE, HD), bf16),
             pltpu.VMEM((QH_HERE, HD), bf16),
             pltpu.VMEM((BLOCKS_HERE, QH_HERE, BLK), f32),
+            pltpu.VMEM((BLOCKS_HERE, 2 * HD, BLK), bf16),
             pltpu.VMEM((BLOCKS_HERE * QH_HERE, HD), bf16),
             pltpu.VMEM((COMB, 16, HD), bf16),
             pltpu.VMEM((POOL, 16, HD), bf16),
@@ -386,7 +420,7 @@
             pltpu.VMEM((HEADS, 8, HD), f32),
             pltpu.VMEM((HEADS, 8, HD), f32),
             pltpu.SemaphoreType.DMA((9,)),
-            dma,
+            pltpu.SemaphoreType.DMA((3,)),
             dma,
             dma,
             dma,

time: 40.6 us -> 39.1 us (0.963)
  Pallas kernels: 39.8 us -> 38.3 us
    pallas_call x1, Pallas kernels: 39.8 us -> 38.3 us  [per_device(): pl.pallas_call(kernel, out_shape=pltpu.VMEM((REQ, 32), f32), in_specs=[hb...]
where the time goes in v3:
time: 39.1 us; the launch traced here: 39 us
  Pallas kernels  38.3 us (98%)
  local copies, waits for them, and re-layouts  0.61 us (2%)
    pallas_call x1, Pallas kernels, per_device(): pl.pallas_call(kernel, out_shape=pltpu.VMEM((REQ, 32), f32), in_specs=[hb...  38.3 us

profile of v3, /device:TPU:1, one launch (start us, length us, event | category | flops | bytes accessed | tf_op | source)
XLA Modules:
  0.0 39.0 jit_solution(425604503729150053)
XLA Ops:
  0.0 38.3 %decode.1 = f32[32,32]{1,0:T(8,128)S(1)} custom-call(bf16[1,2048]{1,0:T(2,128)(2,1)} %q_hbm.1, bf16[1,2,256]{2,1,0:T(2,128)(2,1)} %new_hbm.1, s32[32,32]{1,0:T(8,128)} %tab_hbm.1, s32[32]{0:T(128)} %home_hbm.1, s32[1024]{0:T(1024)} %cnt_hbm.1, s32[32]{0:T(128)} %len_hbm.1, bf16[16,2,2,256,128]{4,3,2,1,0:T(8,128)(2,1)} %cache_hbm.1, bf16[2048,128]{1,0:T(8,128)(2,1)} %w_hbm.1), custom_call_target="tpu_custom_call" | custom-call | tf_op jit(solution)/shard_map/decode/pallas_call | solution.py:393
  38.3 0.6 %copy.10 = f32[32,32]{1,0:T(8,128)} copy(f32[32,32]{1,0:T(8,128)S(1)} %decode.1) | data formatting | bytes 8192

commit v4 on v3

--- a/solution.py
+++ b/solution.py
@@ -33,8 +33,10 @@
 
 
 OFFSETS = pool_offsets()
-RELAYED = (2, Z - 2)
-ROW = {step: row for row, step in enumerate((2, 6, 0, 1, 3, 4, 5, 7))}
+IN_PLANE = [step for step in OFFSETS if step[1] == 0]
+NEAR = (2, 6, 1, 7)
+FAR = (4, 3, 5)
+ROW = {step: row for row, step in enumerate(NEAR + (0,) + FAR)}
 
 
 def shifted(p, step):
@@ -62,7 +64,6 @@
     cache,
     weight,
     q_all,
-    q_mine,
     scores,
     turned,
     o_stack,
@@ -90,7 +91,7 @@
     mine = p // 2
 
     barrier = pltpu.get_barrier_semaphore()
-    for step in OFFSETS:
+    for step in [(0, along, 0) for along in FAR + NEAR] + IN_PLANE:
         pl.semaphore_signal(
             barrier, inc=1, device_id=(shifted(p, step), h), device_id_type=MESH
         )
@@ -129,44 +130,33 @@
     q_rows = jnp.concatenate(
         [q_row[:, i * HD : (i + 1) * HD] for i in range(QH_HERE)], axis=0
     )
+    column = yl * X + x
+    q_mine = q_all.at[column * Z + ROW[0]]
     q_mine[...] = q_rows.astype(jnp.bfloat16)
-    pl.semaphore_wait(barrier, POOL - 1 + HEADS - 1)
-
-    column = yl * X + x
-    for along in RELAYED:
+    pl.semaphore_wait(barrier, Z - 1 + len(IN_PLANE) + HEADS - 1)
+
+    for along in FAR + NEAR:
         pltpu.make_async_remote_copy(
             q_mine,
             q_all.at[column * Z + ROW[Z - along]],
             q_sem.at[0],
-            q_sem.at[2],
+            q_sem.at[3 if along in FAR else 2],
             device_id=(shifted(p, (0, along, 0)), h),
             device_id_type=MESH,
         ).start()
-    for step in OFFSETS:
-        if step[1] not in RELAYED:
+
+    def hand_on(rows):
+        for step in IN_PLANE:
             pltpu.make_async_remote_copy(
-                q_mine,
-                q_all.at[column * Z + ROW[(Z - step[1]) % Z]],
+                rows,
+                rows,
                 q_sem.at[0],
                 q_sem.at[1],
                 device_id=(shifted(p, step), h),
                 device_id_type=MESH,
             ).start()
-    pltpu.make_async_copy(
-        q_mine, q_all.at[column * Z + ROW[0]], q_sem.at[1]
-    ).start()
-    two = q_all.at[pl.ds(column * Z, 2)]
-    pltpu.make_async_copy(two, two, q_sem.at[2]).wait()
-    for step in OFFSETS:
-        if step[1] == 0:
-            pltpu.make_async_remote_copy(
-                two,
-                two,
-                q_sem.at[0],
-                q_sem.at[1],
-                device_id=(shifted(p, step), h),
-                device_id_type=MESH,
-            ).start()
+
+    hand_on(q_mine)
 
     for load in small_loads:
         load.wait()
@@ -208,6 +198,13 @@
 
     own = lax.fori_loop(0, REQ, find_own, jnp.int32(2 * HD))
 
+    near = q_all.at[pl.ds(column * Z, len(NEAR))]
+    pltpu.make_async_copy(near, near, q_sem.at[2]).wait()
+    hand_on(near)
+    far = q_all.at[pl.ds(column * Z + len(NEAR) + 1, len(FAR))]
+    pltpu.make_async_copy(far, far, q_sem.at[3]).wait()
+    hand_on(far)
+
     scale = 1.0 / math.sqrt(HD)
     upper = lax.broadcasted_iota(jnp.int32, (QH_HERE, HD), 0) < 8
     new_kv = new_ref[0].astype(jnp.float32)
@@ -222,7 +219,7 @@
     for b in range(BLOCKS_HERE):
         for i in range(2):
             turned[b, i * HD : (i + 1) * HD, :] = jnp.transpose(cache[b, 0, i])
-    most = q_all.at[pl.ds(0, POOL - 2)]
+    most = q_all.at[pl.ds(0, POOL - Z)]
     whole = pltpu.make_async_copy(most, most, q_sem.at[1])
     whole.wait()
     token = lax.broadcasted_iota(jnp.int32, (QH_HERE, BLK), 1)
@@ -348,7 +345,7 @@
         y_send[i] = jnp.concatenate(
             [y[8 * j : 8 * j + 8, 32 * i : 32 * i + 32] for j in range(4)], axis=1
         )
-    for i in range(1, HEADS):
+    for i in (2, 3, 1):
         pltpu.make_async_remote_copy(
             y_send.at[(h + i) % HEADS],
             y_recv.at[h],
@@ -358,13 +355,6 @@
             device_id_type=MESH,
         ).start()
     pltpu.make_async_copy(y_send.at[h], y_recv.at[h], y_sem.at[1]).start()
-    pltpu.make_async_copy(y_recv, y_recv, y_sem.at[1]).wait()
-    y = (y_recv[0] + y_recv[1]) + (y_recv[2] + y_recv[3])
-    for j in range(4):
-        out_ref[8 * j : 8 * j + 8, :] = y[:, 32 * j : 32 * j + 32]
-
-    three = y_send.at[pl.ds(0, HEADS - 1)]
-    pltpu.make_async_copy(three, three, y_sem.at[0]).wait()
     others = q_all.at[pl.ds(0, POOL - 1)]
     pltpu.make_async_copy(others, others, q_sem.at[0]).wait()
 
@@ -381,6 +371,13 @@
         pltpu.make_async_copy(o_send, o_send, p_sem.at[0]).wait()
         all_s = st_recv.at[pl.ds(0, COMB)]
         pltpu.make_async_copy(all_s, all_s, s_sem.at[0]).wait()
+
+    three = y_send.at[pl.ds(0, HEADS - 1)]
+    pltpu.make_async_copy(three, three, y_sem.at[0]).wait()
+    pltpu.make_async_copy(y_recv, y_recv, y_sem.at[1]).wait()
+    y = (y_recv[0] + y_recv[1]) + (y_recv[2] + y_recv[3])
+    for j in range(4):
+        out_ref[8 * j : 8 * j + 8, :] = y[:, 32 * j : 32 * j + 32]
 
 
 def per_device(
@@ -406,7 +403,6 @@
             pltpu.VMEM((BLOCKS_HERE, 2, 2, BLK, HD), bf16),
             pltpu.VMEM((QH_HERE * HD, HD), bf16),
             pltpu.VMEM((POOL, QH_HERE, HD), bf16),
-            pltpu.VMEM((QH_HERE, HD), bf16),
             pltpu.VMEM((BLOCKS_HERE, QH_HERE, BLK), f32),
             pltpu.VMEM((BLOCKS_HERE, 2 * HD, BLK), bf16),
             pltpu.VMEM((BLOCKS_HERE * QH_HERE, HD), bf16),
@@ -420,7 +416,7 @@
             pltpu.VMEM((HEADS, 8, HD), f32),
             pltpu.VMEM((HEADS, 8, HD), f32),
             pltpu.SemaphoreType.DMA((9,)),
-            pltpu.SemaphoreType.DMA((3,)),
+            pltpu.SemaphoreType.DMA((4,)),
             dma,
             dma,
             dma,

time: 39.1 us -> 37.9 us (0.969)
  Pallas kernels: 38.3 us -> 37.2 us
    pallas_call x1, Pallas kernels: 38.3 us -> 37.2 us  [per_device(): pl.pallas_call(kernel, out_shape=pltpu.VMEM((REQ, 32), f32), in_specs=[hb...]
where the time goes in v4:
time: 37.9 us; the launch traced here: 37.8 us
  Pallas kernels  37.2 us (98%)
  local copies, waits for them, and re-layouts  0.61 us (2%)
    pallas_call x1, Pallas kernels, per_device(): pl.pallas_call(kernel, out_shape=pltpu.VMEM((REQ, 32), f32), in_specs=[hb...  37.2 us

profile of v4, /device:TPU:1, one launch (start us, length us, event | category | flops | bytes accessed | tf_op | source)
XLA Modules:
  0.0 37.8 jit_solution(6432373605613377391)
XLA Ops:
  0.0 37.2 %decode.1 = f32[32,32]{1,0:T(8,128)S(1)} custom-call(bf16[1,2048]{1,0:T(2,128)(2,1)} %q_hbm.1, bf16[1,2,256]{2,1,0:T(2,128)(2,1)} %new_hbm.1, s32[32,32]{1,0:T(8,128)} %tab_hbm.1, s32[32]{0:T(128)} %home_hbm.1, s32[1024]{0:T(1024)} %cnt_hbm.1, s32[32]{0:T(128)} %len_hbm.1, bf16[16,2,2,256,128]{4,3,2,1,0:T(8,128)(2,1)} %cache_hbm.1, bf16[2048,128]{1,0:T(8,128)(2,1)} %w_hbm.1), custom_call_target="tpu_custom_call" | custom-call | tf_op jit(solution)/shard_map/decode/pallas_call | solution.py:390
  37.2 0.6 %copy.10 = f32[32,32]{1,0:T(8,128)} copy(f32[32,32]{1,0:T(8,128)S(1)} %decode.1) | data formatting | bytes 8192

commit v5 on v4

--- a/solution.py
+++ b/solution.py
@@ -34,6 +34,7 @@
 
 OFFSETS = pool_offsets()
 IN_PLANE = [step for step in OFFSETS if step[1] == 0]
+TIERS = ((0,), (1,), (2,), (3,), (7, 6, 5, 4))
 NEAR = (2, 6, 1, 7)
 FAR = (4, 3, 5)
 ROW = {step: row for row, step in enumerate(NEAR + (0,) + FAR)}
@@ -320,15 +321,23 @@
                 jnp.float32
             )
         att_mine[...] = ((sums[0] + sums[1]) + (sums[2] + sums[3])).astype(jnp.bfloat16)
-        for step in OFFSETS:
+        def send_att(step, there):
+            to_yl, to_x = (yl + step[0]) % 2, (x + step[2]) % X
             pltpu.make_async_remote_copy(
                 att_mine,
                 att.at[mine],
                 a_sem.at[0],
                 a_sem.at[1],
-                device_id=(shifted(p, step), h),
+                device_id=(to_yl * 32 + there * X + to_x, h),
                 device_id_type=MESH,
             ).start()
+
+        for tier in TIERS:
+            for step in IN_PLANE:
+                for there in tier:
+                    send_att(step, there)
+            for there in tier:
+                pl.when(z != there)(functools.partial(send_att, (0, 0, 0), there))
         pltpu.make_async_copy(att_mine, att.at[mine], a_sem.at[1]).start()
 
     w_load.wait()

time: 37.9 us -> 37.9 us (level)
  no operation moved by 1% of the time
where the time goes in v5:
time: 37.9 us; the launch traced here: 37.7 us
  Pallas kernels  37.1 us (98%)
  local copies, waits for them, and re-layouts  0.61 us (2%)
    pallas_call x1, Pallas kernels, per_device(): pl.pallas_call(kernel, out_shape=pltpu.VMEM((REQ, 32), f32), in_specs=[hb...  37.1 us

profile of v5, /device:TPU:1, one launch (start us, length us, event | category | flops | bytes accessed | tf_op | source)
XLA Modules:
  0.0 37.7 jit_solution(1872347182433793866)
XLA Ops:
  0.0 37.1 %decode.1 = f32[32,32]{1,0:T(8,128)S(1)} custom-call(bf16[1,2048]{1,0:T(2,128)(2,1)} %q_hbm.1, bf16[1,2,256]{2,1,0:T(2,128)(2,1)} %new_hbm.1, s32[32,32]{1,0:T(8,128)} %tab_hbm.1, s32[32]{0:T(128)} %home_hbm.1, s32[1024]{0:T(1024)} %cnt_hbm.1, s32[32]{0:T(128)} %len_hbm.1, bf16[16,2,2,256,128]{4,3,2,1,0:T(8,128)(2,1)} %cache_hbm.1, bf16[2048,128]{1,0:T(8,128)(2,1)} %w_hbm.1), custom_call_target="tpu_custom_call" | custom-call | tf_op jit(solution)/shard_map/decode/pallas_call | solution.py:399
  37.1 0.6 %copy.10 = f32[32,32]{1,0:T(8,128)} copy(f32[32,32]{1,0:T(8,128)S(1)} %decode.1) | data formatting | bytes 8192
